TPU v7x, 32 devices: a whole 2x2x4 slice. The times are simulated.
32 devices in a mesh: fsdp: 4 (over y, x), blk: 8 (over z, core).
Axes of the slice: x: 2, y: 2, z: 4, core: 2. Of those that a mesh axis runs over, the one named last changes fastest.
Arguments:
- tokens: bfloat16 [12288, 1152], P(('fsdp', 'blk')), may hold values from -6 to 6
- timesteps: int32 [4, 8], P('fsdp'), may hold values from 0 to 999
- segment_ids: int32 [4, 3072], P('fsdp'), may hold values from 0 to 7, as said below
- head_mask: int32 [4, 8, 16], P('fsdp'), may hold values 0 or 1
- chan_mask: int32 [4, 8, 4608], P('fsdp'), may hold values 0 or 1
- token_mask: int32 [12288], P(('fsdp', 'blk')), may hold values 0 or 1
- w_temb: bfloat16 [256, 1152], P('fsdp'), may hold values from -0.375 to 0.375
- w_ada: bfloat16 [1152, 6912], P('fsdp'), may hold values from -0.1875 to 0.1875
- w_qkv: bfloat16 [1152, 3456], P('fsdp'), may hold values from -0.25 to 0.25
- w_out: bfloat16 [1152, 1152], P('fsdp'), may hold values from -1 to 1
- w_fc1: bfloat16 [1152, 4608], P('fsdp'), may hold values from -0.1875 to 0.1875
- w_fc2: bfloat16 [4608, 1152], P('fsdp'), may hold values from -0.1875 to 0.1875
- cotangent: bfloat16 [12288, 1152], P(('fsdp', 'blk')), may hold values from -6 to 6
Outputs:
- result: bfloat16 [12288, 1152], P(('fsdp', 'blk'))
- grad_tokens: bfloat16 [12288, 1152], P(('fsdp', 'blk'))
- grad_temb: float32 [256, 1152], P('fsdp')
- grad_ada: float32 [1152, 6912], P('fsdp')
- grad_qkv: float32 [1152, 3456], P('fsdp')
- grad_out: float32 [1152, 1152], P('fsdp')
- grad_fc1: float32 [1152, 4608], P('fsdp')
- grad_fc2: float32 [4608, 1152], P('fsdp')
Inputs may be any that keep to these rules, and one draw needn't show every extreme that they name: `segment_ids`: in each stream slot 0 holds 1024 tokens, every other slot below 7 holds 1024, 256 or no tokens, and slot 7 holds the remaining padding tokens, at least 128 of them; each slot's tokens are spread over the devices of blk as evenly as possible, their counts on two devices differing by at most one.
All inputs are finite; a program needn't handle non-finite values. No bound on the sum of `head_mask` or of `chan_mask` or of `token_mask` on one device may be relied on, other than what follows from the above.
Results may differ from a plain program's by a relative error of at most 0.022.
Values may be sent and summed in bfloat16 or wider, within the bound.
A program may use at most 256 MiB of HBM per device.

v0:
```python
import functools
import math

import jax
import jax.numpy as jnp
from jax import lax
from jax.experimental import pallas as pl
from jax.experimental.pallas import tpu as pltpu
from jax.sharding import PartitionSpec as P

HIGH = lax.Precision.HIGHEST
BF16 = jnp.bfloat16
F32 = jnp.float32
I32 = jnp.int32
LANES = 128
BLOCK = 256
NEG = -1e30
LOG2E = 1.4426950408889634

VMEM = pl.BlockSpec(memory_space=pltpu.VMEM)
SMEM = pl.BlockSpec(memory_space=pltpu.SMEM)
ANY = pl.BlockSpec(memory_space=pl.ANY)


def shape(dims, kind=BF16):
    return jax.ShapeDtypeStruct(tuple(dims), kind)


def run(name, body, ins, outs, scratch=(), flops=0, vmem=62, collective=None, **more):
    moved = sum(a.size * a.dtype.itemsize for _, a in ins)
    moved += sum(math.prod(o.shape) * jnp.dtype(o.dtype).itemsize for _, o in outs)
    return pl.pallas_call(
        body,
        out_shape=[o for _, o in outs],
        in_specs=[s for s, _ in ins],
        out_specs=[s for s, _ in outs],
        scratch_shapes=list(scratch),
        compiler_params=pltpu.CompilerParams(
            vmem_limit_bytes=vmem << 20,
            collective_id=collective,
            has_side_effects=collective is not None,
        ),
        cost_estimate=pl.CostEstimate(flops=flops, bytes_accessed=moved, transcendentals=0),
        name=name,
        **more,
    )(*[a for _, a in ins])


def swap(array, axis, by):
    size = lax.axis_size(axis)
    return lax.ppermute(array, axis, [(i, i ^ by) for i in range(size)])


def frequencies(steps, entries):
    half = entries // 2
    ladder = jnp.exp(-math.log(10000.0) * lax.iota(jnp.int32, half) / half)
    angles = steps.astype(F32)[:, None] * ladder[None, :]
    return jnp.concatenate([jnp.cos(angles), jnp.sin(angles)], axis=1)


def nn(left, right):
    return lax.dot_general(left, right, (((1,), (0,)), ((), ())), preferred_element_type=F32)


def nt(left, right):
    return lax.dot_general(left, right, (((1,), (1,)), ((), ())), preferred_element_type=F32)


def tn(left, right):
    return lax.dot_general(left, right, (((0,), (0,)), ((), ())), preferred_element_type=F32)


def each(count, step, group=1):
    if count % group:
        group = 1

    def one(index, carry):
        for i in range(group):
            step(index * group + i)
        return carry

    lax.fori_loop(0, count // group, one, 0)


def normal(values):
    center = values - jnp.mean(values, axis=-1, keepdims=True)
    scale = lax.rsqrt(jnp.mean(center * center, axis=-1, keepdims=True) + 1e-06)
    return center * scale, scale


def normal_back(grad, normed, scale):
    along = jnp.mean(grad * normed, axis=-1, keepdims=True)
    return scale * (grad - jnp.mean(grad, axis=-1, keepdims=True) - normed * along)


def flip(index, by):
    bit = 1
    while bit <= by:
        if by & bit:
            index = index + bit * (1 - 2 * ((index // bit) % 2))
        bit *= 2
    return index


def fetch(pairs, sems, first=0):
    copies = []
    for index, (source, target) in enumerate(pairs, first):
        copy = pltpu.make_async_copy(source, target, sems.at[index])
        copy.start()
        copies.append(copy)
    return copies


class Routes:
    def __init__(self, sent, got):
        self.sent, self.got, self.known, self.started = sent, got, {}, []

    def slot(self, name):
        return self.known.setdefault(name, len(self.known))

    def copy(self, name, source, target, to, landed=None):
        return pltpu.make_async_remote_copy(
            src_ref=source,
            dst_ref=target,
            send_sem=self.sent.at[self.slot(name)],
            recv_sem=self.got.at[self.slot(landed or name)],
            device_id=to,
            device_id_type=pl.DeviceIdType.MESH,
        )

    def start(self, name, source, target, to, when=None, landed=None):
        def make():
            return self.copy(name, source, target, to, landed)

        self.started.append((make, when))
        if when is None:
            make().start()
        else:
            pl.when(when)(lambda: make().start())

    def arrive(self, name, target, when=None):
        def wait():
            b = lax.axis_index("blk")
            self.copy(name, target, target, {"blk": b + 1 - 2 * (b % 2)}).wait_recv()

        if when is None:
            wait()
        else:
            pl.when(when)(wait)

    def finish(self):
        for make, when in self.started:
            if when is None:
                make().wait_send()
            else:
                pl.when(when)(lambda make=make: make().wait_send())


def greet(shards, chips):
    f, b = lax.axis_index("fsdp"), lax.axis_index("blk")
    z, c = b // 2, b % 2
    barrier = pltpu.get_barrier_semaphore()

    def signal(to):
        pl.semaphore_signal(barrier, inc=1, device_id=to, device_id_type=pl.DeviceIdType.MESH)

    for k in range(1, shards):
        signal({"fsdp": flip(f, k)})
    signal({"blk": b + 1 - 2 * c})
    pl.when(z > 0)(lambda: signal({"blk": b - 2}))
    pl.when(z < chips - 1)(lambda: signal({"blk": b + 2}))
    ends = (z == 0).astype(I32) + (z == chips - 1).astype(I32)
    pl.semaphore_wait(barrier, shards + 2 - ends)


def greet_all(shards, blocks):
    f, b = lax.axis_index("fsdp"), lax.axis_index("blk")
    barrier = pltpu.get_barrier_semaphore()
    peers = [{"fsdp": flip(f, k)} for k in range(1, shards)]
    peers += [{"blk": flip(b, k)} for k in range(1, blocks)]
    for to in peers:
        pl.semaphore_signal(barrier, inc=1, device_id=to, device_id_type=pl.DeviceIdType.MESH)
    pl.semaphore_wait(barrier, len(peers))


def front_body(
    shards, chips, heads, items_ref, keep_ref, x_ref, c_ref, spec_ref, temb_ref, ada_ref, qkvw_ref,
    outw_ref, fc1w_ref, fc2w_ref, xs_ref, cs_ref, hot_ref, info_ref, mark_ref, perm_ref, mod_ref, cond_ref, low_ref, wave_ref, dm_ref, h_ref,
    qkv_ref, wh_ref, wo_ref, fc2_ref, *refs,
):
    fc_refs, refs = refs[:-19], refs[-19:]
    x_all, spec_all, temb_all, part_own, part_got, mod_all, hots, dms, wh_all, wo_all = refs[:10]
    h_all, ada_s, qkvw_s, fc1_s, fc_all, local, loads, sent, got = refs[10:]
    f, b = lax.axis_index("fsdp"), lax.axis_index("blk")
    z, c = b // 2, b % 2
    blocks = 2 * chips
    pair = b + 1 - 2 * c
    width = BLOCK // blocks
    count, size = x_ref.shape
    units = count // width
    own = heads // blocks
    head_size = size // heads
    slots = spec_ref.shape[0]
    routes = Routes(sent, got)
    down = fc2_ref.shape[0]
    inside = fetch(
        [
            (ada_ref, ada_s),
            (qkvw_ref, qkvw_s),
            (outw_ref, wo_all.at[f]),
            (fc1w_ref, fc1_s),
            (fc2w_ref.at[pl.ds(pl.multiple_of(c * down, 16), down)], fc2_ref),
        ],
        loads,
    )
    greet(shards, chips)

    spec_all[f] = spec_ref[...]
    temb_all[f] = temb_ref[...]
    for k in range(1, shards):
        to = {"fsdp": flip(f, k)}
        routes.start(("spec", k), spec_ref, spec_all.at[f], to)
        routes.start(("temb", k), temb_ref, temb_all.at[f], to)

    items = items_ref[...]
    slot = lax.broadcasted_iota(I32, (slots, count), 0)
    hot = (items == slot).astype(F32)
    start = jnp.sum((items < slot).astype(F32), axis=1, keepdims=True)
    end = start + jnp.sum(hot, axis=1, keepdims=True)
    row = lax.broadcasted_iota(I32, (count, count), 0)
    col = lax.broadcasted_iota(I32, (count, count), 1)
    rank = nn(hot.astype(BF16), (row <= col).astype(BF16))
    place = jnp.sum(hot * (start + rank), axis=0, keepdims=True) - 1.0
    perm = (row.astype(F32) == place).astype(BF16)
    perm_ref[...] = perm
    x_s = nn(perm, x_ref[...]).astype(BF16)
    xs_ref[...] = x_s
    x_all[b] = x_s

    def line(side, s, send):
        away = s - 1 if send else s
        chip = z - away if side == 0 else z + away
        ahead = z + 1 < chips if side == 0 else z > 0
        known = z >= away if side == 0 else z + away < chips
        when = known & ahead if send else known
        return chip * 2 + c, {"blk": b + 2 if side == 0 else b - 2}, when

    def send_on(s):
        for side in range(2):
            device, to, when = line(side, s, True)
            routes.start(("line", side, s), x_all.at[device], x_all.at[device], to, when)

    send_on(1)
    routes.start("pair", x_all.at[b], x_all.at[b], {"blk": pair})
    cs_ref[...] = nn(perm, c_ref[...]).astype(BF16)
    keep = jnp.broadcast_to(keep_ref[...].astype(F32), (slots, count)).astype(BF16)
    kept = nt(keep, perm)
    at = lax.broadcasted_iota(I32, (slots, count), 1).astype(F32)
    hots[0] = kept * ((at >= start) & (at < end)).astype(F32)
    first = (lax.broadcasted_iota(I32, (slots, LANES), 1) * width).astype(F32)
    mine = ((first >= start) & (first < end)).astype(F32)
    mark_ref[...] = mine
    which = lax.broadcasted_iota(I32, (slots, LANES), 0).astype(F32)
    info_ref[0:1, :] = jnp.sum(mine * which, axis=0, keepdims=True).astype(I32)
    info_ref[1:2, :] = (jnp.sum(mine * start, axis=0, keepdims=True) / width).astype(I32)
    info_ref[2:3, :] = (jnp.sum(mine * end, axis=0, keepdims=True) / width).astype(I32)
    info_ref[3:8, :] = jnp.zeros((5, LANES), I32)

    for k in range(1, shards):
        other = flip(f, k)
        routes.arrive(("spec", k), spec_all.at[other])
        routes.arrive(("temb", k), temb_all.at[other])
    spectra = spec_all[...].reshape(shards * slots, -1).astype(BF16)
    condition = nn(spectra, temb_all[...].reshape(-1, size))
    rows = ada_ref.shape[0]
    for shard in range(shards):

        @pl.when(f == shard)
        def _():
            cond_ref[...] = condition[:, shard * rows : (shard + 1) * rows]
            freqs = temb_ref.shape[0]
            wave_ref[...] = spectra[:, shard * freqs : (shard + 1) * freqs].astype(F32)

    values = cond_ref[...]
    lifted = (values / (1.0 + jnp.exp(-values))).astype(BF16)
    low_ref[...] = lifted
    inside[0].wait()
    for side in range(2):
        columns = slice(side * 3 * size, (side + 1) * 3 * size)
        found = nn(lifted, ada_s[:, columns])
        part_own[:, side] = found.reshape(shards, slots, 3 * size)
    for k in range(1, shards):
        other = flip(f, k)
        routes.start(("part", k), part_own.at[other, c], part_got.at[k], {"fsdp": other})

    rows = qkvw_ref.shape[0]
    inside[1].wait()
    narrow = own * head_size
    row = lax.broadcasted_iota(I32, (size, 2 * LANES), 0)
    col = lax.broadcasted_iota(I32, (size, 2 * LANES), 1)
    pick = ((row == b * narrow + col) & (col < narrow)).astype(F32).astype(BF16)
    wh_all[f] = jnp.concatenate(
        [
            nn(qkvw_s[:, part * size : (part + 1) * size], pick)[:, 0:narrow]
            for part in range(3)
        ],
        axis=1,
    ).astype(BF16)
    if shards == 4:
        for k in (1, 2):
            routes.start(("head", k), wh_all.at[f], wh_all.at[f], {"fsdp": flip(f, k)})
    else:
        for k in range(1, shards):
            routes.start(("head", k), wh_all.at[f], wh_all.at[f], {"fsdp": flip(f, k)})

    def take(s):
        for side in range(2):
            device, _, when = line(side, s, False)
            routes.arrive(("line", side, s), x_all.at[device], when)
            if s + 1 < chips:
                device, to, onward = line(side, s + 1, True)
                routes.start(
                    ("line", side, s + 1), x_all.at[device], x_all.at[device], to, onward
                )
            device, _, when = line(side, s, False)
            routes.start(
                ("pair", side, s), x_all.at[device], x_all.at[device], {"blk": pair}, when
            )

    take(1)
    if shards == 4:
        half = rows // 2
        for k, low in ((1, 0), (2, half)):
            routes.arrive(("head", k), wh_all.at[flip(f, k)])
            part = wh_all.at[flip(f, k), low : low + half]
            routes.start(("head", 3, k), part, part, {"fsdp": flip(f, 3 - k)})

    cut = size // (2 * LANES) * LANES
    for k in range(1, 3 if shards == 4 else shards):
        routes.start(("out", k), outw_ref.at[c], wo_all.at[f, c], {"fsdp": flip(f, k)})

    blocks_fc = fc_all.shape[1]
    part = fc1_s.shape[1] // shards // 2
    inside[3].wait()
    for core in range(2):

        @pl.when(c == core)
        def _():
            picked = jnp.concatenate(
                [
                    fc1_s[:, (2 * shard + core) * part : (2 * shard + core + 1) * part]
                    for shard in range(shards)
                ],
                axis=1,
            )
            for block_at in range(blocks_fc):
                fc_all[0, block_at] = picked[:, block_at * size : (block_at + 1) * size]

    for k in range(1, len(fc_refs)):
        routes.start(("fc", k), fc_all.at[0], fc_all.at[k], {"fsdp": flip(f, k)})

    total = part_own[f, c]
    for k in range(1, shards):
        routes.arrive(("part", k), part_got.at[k])
        total = total + part_got[k]
    mod_all[c] = total
    routes.start("mod", mod_all.at[c], mod_all.at[c], {"blk": pair})
    routes.arrive("mod", mod_all.at[1 - c])
    total = jnp.concatenate([mod_all[0], mod_all[1]], axis=1)
    mod_ref[...] = lax.dot_general(
        mine[:, : mod_ref.shape[0]], total, (((0,), (0,)), ((), ())), precision=HIGH,
        preferred_element_type=F32,
    )

    def early(u):
        rows = pl.ds(pl.multiple_of(u * width, width), width)
        gate = mod_ref[pl.ds(u, 1), 5 * size : 6 * size]
        dms[0, rows, :] = (cs_ref[rows, :].astype(F32) * gate).astype(BF16)

    each(units, early)
    routes.start("dm", dms.at[0], dms.at[1], {"blk": pair})
    routes.start("hot", hots.at[0], hots.at[1], {"blk": pair})

    if shards == 4:
        half = rows // 2
        routes.arrive(("head", 3, 1), wh_all.at[flip(f, 3), 0:half])
        routes.arrive(("head", 3, 2), wh_all.at[flip(f, 3), half:rows])
    else:
        for k in range(1, shards):
            routes.arrive(("head", k), wh_all.at[flip(f, k)])
    packed = wh_all[...].reshape(size, 3 * narrow)
    wh_ref[...] = jnp.zeros_like(wh_ref)
    for i in range(3 * own):
        wh_ref[:, i * LANES : i * LANES + head_size] = packed[
            :, i * head_size : (i + 1) * head_size
        ]

    def block(device):
        at = pl.ds(pl.multiple_of(device * width, width), width)

        def one(u):
            shift = mod_ref[pl.ds(u, 1), 0:size]
            scale = mod_ref[pl.ds(u, 1), size : 2 * size]
            part = x_all[device, pl.ds(pl.multiple_of(u * width, width), width), :]
            normed, _ = normal(part.astype(F32))
            low = (normed * (1.0 + scale) + shift).astype(BF16)
            h_all[pl.ds(pl.multiple_of(u * width, width), width), :] = low

        each(units, one, 3)
        copies = fetch(
            [
                (h_all.at[u * width : (u + 1) * width], h_ref.at[u, at])
                for u in range(units)
            ],
            local,
        )
        found = nn(h_all[...], wh_ref[...]).astype(BF16)
        qkv_ref[:, at, :] = found.reshape(units, width, found.shape[1])
        for copy in copies:
            copy.wait()

    routes.arrive("pair", x_all.at[pair])
    each(2, lambda core: block(z * 2 + core))

    def work(s):
        for side in range(2):
            device, _, when = line(side, s, False)
            routes.arrive(("pair", side, s), x_all.at[device + 1 - 2 * c], when)

        def pick(q):
            chip = z - s + 2 * s * (q // 2)

            @pl.when((chip >= 0) & (chip < chips))
            def _():
                block(chip * 2 + q % 2)

        each(4, pick)

    for s in range(2, chips):
        take(s)
        if s == 2:
            for k in range(1, 3 if shards == 4 else shards):
                other = flip(f, k)
                routes.arrive(("out", k), wo_all.at[other, c])
                if shards == 4:
                    columns = slice(0, cut) if k == 1 else slice(cut, size)
                    piece = wo_all.at[other, c, :, columns]
                    routes.start(("out", 3, k), piece, piece, {"fsdp": flip(f, 3 - k)})
                routes.start(
                    ("pair out", k), wo_all.at[other, c], wo_all.at[other, c], {"blk": pair}
                )
        work(s - 1)
    if shards == 4:
        other = flip(f, 3)
        routes.arrive(("out", 3, 1), wo_all.at[other, c, :, 0:cut])
        routes.arrive(("out", 3, 2), wo_all.at[other, c, :, cut:size])
        routes.start(("pair out", 3), wo_all.at[other, c], wo_all.at[other, c], {"blk": pair})
    work(chips - 1)
    inside[2].wait()
    for k in range(1, len(fc_refs)):
        routes.arrive(("fc", k), fc_all.at[k])
    inside[4].wait()
    for k in range(1, shards):
        routes.arrive(("pair out", k), wo_all.at[flip(f, k), 1 - c])
    routes.arrive("dm", dms.at[1])
    routes.arrive("hot", hots.at[1])
    routes.finish()
    copies = fetch(
        [(wo_all, wo_ref), (dms, dm_ref), (hots, hot_ref)]
        + [(fc_all.at[k], ref) for k, ref in enumerate(fc_refs)],
        local,
    )
    for copy in copies:
        copy.wait()


def exchange_lanes(tiles, width):
    tiles = list(tiles)
    count = len(tiles)
    group = lax.broadcasted_iota(I32, tiles[0].shape, 1) // width
    half = count // 2
    while half:
        low = (group // half) % 2 == 0
        fresh = list(tiles)
        for i in range(count):
            if (i // half) % 2 == 0:
                a, d = tiles[i], tiles[i + half]
                fresh[i] = jnp.where(low, a, pltpu.roll(d, half * width, 1))
                fresh[i + half] = jnp.where(low, pltpu.roll(a, LANES - half * width, 1), d)
        tiles = fresh
        half //= 2
    return tiles


def in_groups(first, last, sizes, step, carry):
    for size in sizes:
        count = (last - first) // size

        def one(index, carry, first=first, size=size):
            return step(first + index * size, size, carry)

        carry = lax.fori_loop(0, count, one, carry)
        first = first + count * size
    return carry


def attend_body(
    own, size, blocks, ids_ref, info_ref, mask_ref, qkv_ref, o_ref, lse_ref, out_ref, held, turned, placed
):
    units = qkv_ref.shape[0]
    width = BLOCK // blocks
    b = ids_ref[1]
    scale = LOG2E / math.sqrt(size)
    tall = turned.shape[2]

    def turn(j):
        for h in range(own):
            at = (2 * own + h) * LANES
            values = qkv_ref[j, :, at : at + LANES].astype(F32).T
            turned[j, h] = values[0:tall].astype(BF16)

    each(units, turn, 2)

    def one_unit(u):
        queries = [qkv_ref[u, :, h * LANES : (h + 1) * LANES] for h in range(own)]

        def some_blocks(j, count, carry):
            fresh = []
            for h in range(own):
                top, total, acc = carry[h]
                keys = qkv_ref[pl.ds(j, count), :, (own + h) * LANES : (own + h + 1) * LANES]
                scores = nt(keys.reshape(count * BLOCK, LANES), queries[h]) * scale
                new_top = jnp.maximum(top, jnp.max(scores, axis=0, keepdims=True))
                probs = jnp.exp2(scores - new_top)
                decay = jnp.exp2(top - new_top)
                total = total * decay + jnp.sum(probs, axis=0, keepdims=True)
                acc = acc * decay
                low = probs.astype(BF16)
                for i in range(count):
                    acc = acc + nn(turned[j + i, h], low[i * BLOCK : (i + 1) * BLOCK])
                fresh.append((new_top, total, acc))
            return tuple(fresh)

        start = tuple(
            (
                jnp.full((1, BLOCK), NEG, F32),
                jnp.zeros((1, BLOCK), F32),
                jnp.zeros((tall, BLOCK), F32),
            )
            for _ in range(own)
        )
        done = in_groups(info_ref[1, u], info_ref[2, u], (4, 2, 1), some_blocks, start)
        slot = info_ref[0, u]
        rows = []
        for h in range(own):
            top, total, acc = done[h]
            keep = mask_ref[slot, b * own + h].astype(F32)
            rows.append((acc * (keep / total))[0:size])
            lse_ref[u, h : h + 1, :] = top + jnp.log2(total)
        held[u] = jnp.concatenate(rows, axis=0) if own > 1 else rows[0]
        o_ref[u] = held[u].astype(BF16)

    each(units, one_unit)
    groups = LANES // width
    for g in range(units // groups):
        for e in range(blocks // groups):
            tiles = [
                held[groups * g + i, :, e * LANES : (e + 1) * LANES] for i in range(groups)
            ]
            for j, tile in enumerate(exchange_lanes(tiles, width)):
                placed[groups * e + j, :, g * LANES : (g + 1) * LANES] = tile.astype(BF16)
    for k in range(blocks):
        out_ref[k] = placed[lax.bitwise_xor(b, k)]


def attend_back_body(
    own, size, blocks, ids_ref, info_ref, mask_ref, qkv_ref, o_ref, lse_ref, given, d_ref, up, delta, d_q,
    d_k, d_v,
):
    units = qkv_ref.shape[0]
    width = BLOCK // blocks
    b = ids_ref[1]
    factor = 1.0 / math.sqrt(size)
    scale = LOG2E * factor
    up[...] = jnp.zeros_like(up)
    groups = LANES // width
    for g in range(units // groups):
        for e in range(blocks // groups):
            tiles = [
                given[groups * e + j, :, g * LANES : (g + 1) * LANES].astype(F32)
                for j in range(groups)
            ]
            for i, tile in enumerate(exchange_lanes(tiles, width)):
                unit = groups * g + i
                slot = info_ref[0, unit]
                for h in range(own):
                    keep = mask_ref[slot, b * own + h].astype(F32)
                    kept = tile[h * size : (h + 1) * size] * keep
                    up[unit, h, 0:size, e * LANES : (e + 1) * LANES] = kept.astype(BF16)
                    mine = o_ref[unit, h * size : (h + 1) * size, e * LANES : (e + 1) * LANES]
                    delta[unit, h : h + 1, e * LANES : (e + 1) * LANES] = jnp.sum(
                        kept * mine.astype(F32), axis=0, keepdims=True
                    )
    d_q[...] = jnp.zeros_like(d_q)

    def one_unit(j):
        d_k[...] = jnp.zeros_like(d_k)
        d_v[...] = jnp.zeros_like(d_v)
        keys = [qkv_ref[j, :, (own + h) * LANES : (own + h + 1) * LANES] for h in range(own)]
        turned = [keys[h].astype(F32).T.astype(BF16) for h in range(own)]

        def some_blocks(i, count, carry):
            for h in range(own):
                at = (2 * own + h) * LANES
                values = qkv_ref[j, :, at : at + LANES]
                sum_k = sum_v = 0.0
                for n in range(count):
                    queries = qkv_ref[i + n, :, h * LANES : (h + 1) * LANES]
                    scores = nt(keys[h], queries) * scale
                    probs = jnp.exp2(scores - lse_ref[i + n, h : h + 1, :])
                    d_probs = nn(values, up[i + n, h])
                    d_scores = (probs * (d_probs - delta[i + n, h : h + 1, :])).astype(BF16)
                    sum_k = sum_k + nn(d_scores, queries)
                    sum_v = sum_v + nt(probs.astype(BF16), up[i + n, h])
                    d_q[i + n, h] += nn(turned[h], d_scores)
                d_k[h] += sum_k
                d_v[h] += sum_v
            return carry

        in_groups(info_ref[1, j], info_ref[2, j], (4, 2, 1), some_blocks, 0)
        for h in range(own):
            at = (own + h) * LANES
            d_ref[j, :, at : at + LANES] = (d_k[h] * factor).astype(BF16)
            at = (2 * own + h) * LANES
            d_ref[j, :, at : at + LANES] = d_v[h].astype(BF16)

    each(units, one_unit)

    def turn(i):
        for h in range(own):
            d_ref[i, :, h * LANES : (h + 1) * LANES] = (d_q[i, h].T * factor).astype(BF16)

    each(units, turn)


def project_body(shards, blocks, moves, mod_ref, x_ref, w_ref, p_ref, *refs):
    sources, refs = refs[: len(moves)], refs[len(moves) :]
    attn_ref, x1_ref, h_ref, om_ref = refs[:4]
    landed, (om_all, h_all, local, sent, got) = refs[4 : 4 + len(moves)], refs[4 + len(moves) :]
    f, b = lax.axis_index("fsdp"), lax.axis_index("blk")
    width = BLOCK // blocks
    size = x_ref.shape[1]
    routes = Routes(sent, got)
    greet_all(shards, blocks)
    for k in range(blocks - 1, 0, -1):
        routes.start(("om", k), p_ref.at[k], om_all.at[b], {"blk": flip(b, k)})
    for i, (first, high, k) in enumerate(moves):
        routes.start(("move", i), sources[i].at[first:high], landed[i], {"fsdp": flip(f, k)})
    om_all[b] = p_ref[0]
    for k in range(1, blocks):
        routes.arrive(("om", k), om_all.at[flip(b, k)])
    om = om_all[...].reshape(size, x_ref.shape[0])
    om_ref[...] = om
    weight = w_ref[...]
    attn_ref[...] = tn(om, weight)

    def one(u):
        rows = pl.ds(pl.multiple_of(u * width, width), width)
        gate, shift, scale = [mod_ref[pl.ds(u, 1), i * size : (i + 1) * size] for i in (2, 3, 4)]
        middle = x_ref[rows, :].astype(F32) + gate * attn_ref[rows, :]
        x1_ref[rows, :] = middle
        normed, _ = normal(middle)
        h_all[0, rows, :] = (normed * (1.0 + scale) + shift).astype(BF16)

    each(x_ref.shape[0] // width, one, 3)
    routes.start("h", h_all.at[0], h_all.at[1], {"blk": flip(b, 1)})
    routes.arrive("h", h_all.at[1])
    copy = pltpu.make_async_copy(h_all, h_ref, local.at[0])
    copy.start()
    for i in range(len(moves)):
        routes.arrive(("move", i), landed[i])
    routes.finish()
    copy.wait()


def ff_body(shards, step, sides, plan1, plan2, ids_ref, hot_ref, chan_ref, h_ref, dm_ref, *refs):
    w1_refs, refs = refs[: len(plan1)], refs[len(plan1) :]
    w2_refs, refs = refs[: len(plan2)], refs[len(plan2) :]
    f = ids_ref[0]
    mlp_m, mlp_o, dh_m, dh_o, g_ref, w1, w2, h, dm, turned, hid_s, du_s, mlp, dh, g1, g2, sems = refs
    total = h.shape[0]
    count = total // 2
    f_size, size = w2.shape
    blocks = f_size // size
    row1, row2 = size // shards, f_size // shards

    def up_part(ref, shard, low, high):
        block = low // size
        return ref.at[
            shard, block * row1 : (block + 1) * row1, low - block * size : high - block * size
        ]

    def down_part(ref, shard, low, high):
        at = blocks * row1 - shard * row2
        return ref.at[shard, at + low : at + high]

    def chunk(index):
        low, high = index * step, (index + 1) * step
        cols = [
            (max(low, i * size), min(high, (i + 1) * size))
            for i in range(blocks)
            if max(low, i * size) < min(high, (i + 1) * size)
        ]
        rows = [
            (i, max(low, i * row2), min(high, (i + 1) * row2))
            for i in range(shards)
            if max(low, i * row2) < min(high, (i + 1) * row2)
        ]
        return cols, rows

    used = [0]

    def begin(pairs):
        copies = fetch(pairs, sems, used[0])
        used[0] += len(copies)
        return copies

    waits = [
        begin(
            [
                (h_ref.at[0], h.at[0:count]),
                (h_ref.at[1], h.at[count:total]),
                (dm_ref.at[0], dm.at[0:count]),
                (dm_ref.at[1], dm.at[count:total]),
            ]
        )
    ]
    chunks = f_size // step
    pairs = [[] for _ in range(chunks)]
    for ref, (k, first) in zip(w1_refs, plan1):
        at = pl.ds(pl.multiple_of(lax.bitwise_xor(f, k) * row1, 16), row1)
        for i in range(ref.shape[0]):
            low = (first + i) * size
            pairs[low // step].append((ref.at[i], w1.at[at, low : low + size]))
    for ref, (k, first) in zip(w2_refs, plan2):
        at = pl.multiple_of(lax.bitwise_xor(f, k) * row2 + first, 16)
        pairs[0].append((ref, w2.at[pl.ds(at, ref.shape[0])]))
    waits += [begin(some) for some in pairs]
    for copy in waits[0]:
        copy.wait()
    for at in range(0, total, LANES):
        turned[:, at : at + LANES] = h[at : at + LANES, :].astype(F32).T.astype(BF16)
    hots = jnp.concatenate([hot_ref[side] for side in range(2)], axis=1).astype(BF16)
    left = []
    for index in range(chunks):
        for copy in waits[index + 1]:
            copy.wait()
        cols = slice(index * step, (index + 1) * step)
        up = w1[:, cols]
        down = w2[cols, :]
        chan = chan_ref[:, cols].astype(F32).astype(BF16)
        for side in range(sides):
            rows = slice(side * total // sides, (side + 1) * total // sides)
            keep = tn(hots[:, rows], chan)
            pre = nn(h[rows, :], up)
            inner = pre * pre
            bent = jnp.tanh(0.7978845608028654 * (pre + 0.044715 * inner * pre))
            half = 0.5 * (1.0 + bent)
            hid = (pre * half * keep).astype(BF16)
            slope = half + (0.5 * 0.7978845608028654) * pre * (1.0 - bent * bent) * (
                1.0 + (3.0 * 0.044715) * inner
            )
            back = nt(dm[rows, :], down)
            du = (slope * back * keep).astype(BF16)
            hid_s[rows, :] = hid
            du_s[rows, :] = du
            if index:
                mlp[rows, :] += nn(hid, down)
                dh[rows, :] += nt(du, up)
            else:
                mlp[rows, :] = nn(hid, down)
                dh[rows, :] = nt(du, up)
        g1[:, cols] = nn(turned[...], du_s[...]).astype(BF16)
        g2[cols, :] = tn(hid_s[...], dm[...]).astype(BF16)
        parts, rows = chunk(index)
        pairs = [
            (g1.at[shard * row1 : (shard + 1) * row1, lo:hi], up_part(g_ref, shard, lo, hi))
            for shard in range(shards)
            for lo, hi in parts
        ]
        pairs += [(g2.at[lo:hi], down_part(g_ref, shard, lo, hi)) for shard, lo, hi in rows]
        left += begin(pairs)
    mlp_m[...] = mlp[0:count, :]
    mlp_o[...] = mlp[count:total, :].astype(BF16)
    dh_m[...] = dh[0:count, :]
    dh_o[...] = dh[count:total, :].astype(BF16)
    for copy in left:
        copy.wait()


def middle_body(
    shards, blocks, mod_ref, mark_ref, x1_ref, c_ref, dh_ref, dho_ref, mlp_ref, mlpo_ref, attn_ref, om_ref,
    w_ref, perm_ref, up_ref, dx_ref, two_ref, gate_ref, r_ref, mine_ref, other_ref, dh_in, mlp_in, da, leave,
    up_all, held, grad, by_unit, w_s, mlp_s, attn_s, om_s, local, sent, got,
):
    f, b = lax.axis_index("fsdp"), lax.axis_index("blk")
    c = b % 2
    width = BLOCK // blocks
    count, size = x1_ref.shape
    units = count // width
    routes = Routes(sent, got)
    inside = fetch([(w_ref, w_s), (mlp_ref, mlp_s), (attn_ref, attn_s), (om_ref, om_s)], local)
    greet_all(shards, blocks)
    routes.start("dh", dho_ref, dh_in, {"blk": flip(b, 1)})
    routes.start("mlp", mlpo_ref, mlp_in, {"blk": flip(b, 1)})
    by_unit[...] = jnp.zeros_like(by_unit)
    routes.arrive("dh", dh_in)

    def one(u):
        rows = pl.ds(pl.multiple_of(u * width, width), width)
        gate = mod_ref[pl.ds(u, 1), 2 * size : 3 * size]
        scale = mod_ref[pl.ds(u, 1), 4 * size : 5 * size]
        normed, spread = normal(x1_ref[rows, :])
        grad = dh_ref[rows, :] + dh_in[rows, :].astype(F32)
        by_unit[pl.ds(u, 1), 0:size] = jnp.sum(grad, axis=0, keepdims=True)
        by_unit[pl.ds(u, 1), size : 2 * size] = jnp.sum(grad * normed, axis=0, keepdims=True)
        dx = c_ref[rows, :].astype(F32) + normal_back(grad * (1.0 + scale), normed, spread)
        dx_ref[rows, :] = dx
        da[rows, :] = (dx * gate).astype(BF16)

    each(units, one, 3)
    inside[0].wait()
    for k in range(blocks - 1, -1, -1):
        piece = nt(w_s[flip(b, k)], da[...]).astype(BF16)
        if k:
            leave[k] = piece
            routes.start(("up", k), leave.at[k], up_all.at[b], {"blk": flip(b, k)})
        else:
            up_all[b] = piece

    def over_slots(target):
        target[...] = lax.dot_general(
            mark_ref[:, : by_unit.shape[0]], by_unit[...], (((1,), (0,)), ((), ())), precision=HIGH,
            preferred_element_type=F32,
        )

    over_slots(two_ref)
    routes.arrive("mlp", mlp_in)
    for copy in inside[1:]:
        copy.wait()

    def two(u):
        rows = pl.ds(pl.multiple_of(u * width, width), width)
        gate = mod_ref[pl.ds(u, 1), 5 * size : 6 * size]
        mlp = mlp_s[rows, :] + mlp_in[rows, :].astype(F32)
        held[rows, :] = (x1_ref[rows, :] + gate * mlp).astype(BF16)
        by_unit[pl.ds(u, 1), 0:size] = jnp.sum(
            dx_ref[rows, :] * attn_s[rows, :], axis=0, keepdims=True
        )
        by_unit[pl.ds(u, 1), size : 2 * size] = jnp.sum(
            c_ref[rows, :].astype(F32) * mlp, axis=0, keepdims=True
        )

    each(units, two, 3)
    over_slots(gate_ref)
    r_ref[...] = tn(perm_ref[...], held[...]).astype(BF16)
    grad[...] = nn(om_s[...], da[...]).astype(BF16).reshape(grad.shape)
    for k in range(shards):
        base = 2 * flip(f, k)
        mine_ref[k] = grad[base + c]
        other_ref[k] = grad[base + 1 - c]
    for k in range(1, blocks):
        routes.arrive(("up", k), up_all.at[flip(b, k)])
    up_ref[...] = up_all[...]
    routes.finish()


def stream_back_body(
    shards, chips, heads, per, h_ref, gs_ref, d_ref, wh_ref, mod_ref, mine_ref, x_ref, dx_ref, perm_ref,
    gm_ref, o_ref, sum_ref, g_ref, go_ref, give, take, keep, came, h_s, acc, low, others, out_in, out_low,
    out_got, total, held, by_unit, local, sent, got,
):
    f, b = lax.axis_index("fsdp"), lax.axis_index("blk")
    z, c = b // 2, b % 2
    pair = b + 1 - 2 * c
    width = BLOCK // (2 * chips)
    units = d_ref.shape[0]
    count, size = x_ref.shape
    wide = wh_ref.shape[1]
    own = heads // (2 * chips)
    head_size = size // heads
    rows = low.shape[1]
    steps = units // per
    routes = Routes(sent, got)

    def load(i):
        return pltpu.make_async_copy(
            h_ref.at[pl.ds(i * per, per)], h_s.at[i % 2], local.at[i % 2]
        )

    load(0).start()
    greet(shards, chips)
    routes.start("out", gs_ref, out_in, {"blk": pair})

    def partial(device, target):
        at = pl.ds(pl.multiple_of(device * width, width), width)
        grads = d_ref[:, at, :].reshape(count, wide)
        for col in range(0, size, 3 * LANES):
            target[:, col : col + 3 * LANES] = nt(
                grads, wh_ref[col : col + 3 * LANES, :]
            ).astype(BF16)

    def route(side, t):
        if side == 0:
            chip = chips - 1 - t
            return chip, z < chip, z > 0
        return t, z > t, z < chips - 1

    def onward(side, t, chip, when):
        if side == 0:
            slot, to = chip, b + 2
        else:
            slot, to = chip + (chips - chip) * (z - 1 == chip).astype(I32), b - 2
        routes.start(("sum", side, t), keep.at[chip], came.at[slot], {"blk": to}, when)

    def join(chip, slot=None):
        value = keep[chip].astype(F32) + take[chip].astype(F32)
        if slot is not None:
            value = value + came[slot].astype(F32)
        keep[chip] = value.astype(BF16)

    for t in range(chips - 1):
        for side in range(2):
            chip, passes, inside = route(side, t)

            @pl.when(passes)
            def _():
                partial(chip * 2 + 1 - c, give.at[chip])

            routes.start(("pair", side, t), give.at[chip], take.at[chip], {"blk": pair}, passes)

            @pl.when(passes)
            def _():
                partial(chip * 2 + c, keep.at[chip])

            first = passes & jnp.logical_not(inside)
            routes.arrive(("pair", side, t), take.at[chip], first)

            pl.when(first)(lambda: join(chip))
            onward(side, t, chip, first)

    partial(z * 2 + 1 - c, give.at[z])
    routes.start(("pair", "own"), give.at[z], take.at[z], {"blk": pair})
    partial(z * 2 + c, keep.at[z])

    def gather(i):
        if i + 1 < steps:
            load(i + 1).start()
        load(i).wait()
        part = tn(
            h_s[i % 2].reshape(per * BLOCK, size),
            d_ref[i * per : (i + 1) * per].reshape(per * BLOCK, wide),
        )
        if i:
            acc[...] += part
        else:
            acc[...] = part

    for t in range(max(chips - 1, steps)):
        if t < steps:
            gather(t)
        if t == steps - 1:
            packed = jnp.concatenate(
                [acc[:, i * LANES : i * LANES + head_size] for i in range(3 * own)], axis=1
            )
            low[...] = packed.astype(BF16).reshape(low.shape)
            for k in range(1, shards):
                other = flip(f, k)
                routes.start(("grad", k), low.at[other], others.at[k], {"fsdp": other})
        if t == 0:
            routes.arrive("out", out_in)
            out_low[...] = (gm_ref[...].astype(F32) + out_in[...].astype(F32)).astype(BF16)
            for k in range(1, shards):
                routes.start(("out", k), out_low.at[k], out_got.at[k], {"fsdp": flip(f, k)})
        if t >= chips - 1:
            continue
        for near, side in ((True, 0), (True, 1), (False, 1), (False, 0)):
            chip, passes, inside = route(side, t)
            when = passes & inside & ((z < chips // 2) == near)
            routes.arrive(("pair", side, t), take.at[chip], when)
            routes.arrive(("sum", side, t), came.at[chip], when)
            pl.when(when)(lambda: join(chip, chip))
            onward(side, t, chip, when)

    grad, grad_out = low[f].astype(F32), out_low[0].astype(F32)
    for k in range(1, shards):
        routes.arrive(("grad", k), others.at[k])
        grad = grad + others[k].astype(F32)
        routes.arrive(("out", k), out_got.at[k])
        grad_out = grad_out + out_got[k].astype(F32)
    g_ref[...] = grad.astype(BF16)
    go_ref[...] = grad_out.astype(BF16)

    routes.arrive(("pair", "own"), take.at[z])
    total[...] = keep[z].astype(F32) + take[z].astype(F32)
    for t in range(chips - 1):
        for side in range(2):
            chip, _, inside = route(side, t)
            slot = chip if side == 0 else chips
            here = (z == chip) & inside
            routes.arrive(("sum", side, t), came.at[slot], here)

            @pl.when(here)
            def _():
                total[...] += came[slot].astype(F32)

    by_unit[...] = jnp.zeros_like(by_unit)

    def one(u):
        rows = pl.ds(pl.multiple_of(u * width, width), width)
        scale = mod_ref[pl.ds(u, 1), size : 2 * size]
        normed, spread = normal(x_ref[rows, :].astype(F32))
        grad = total[rows, :]
        by_unit[pl.ds(u, 1), 0:size] = jnp.sum(grad, axis=0, keepdims=True)
        by_unit[pl.ds(u, 1), size : 2 * size] = jnp.sum(grad * normed, axis=0, keepdims=True)
        dx = dx_ref[rows, :] + normal_back(grad * (1.0 + scale), normed, spread)
        held[rows, :] = dx.astype(BF16)

    each(units, one, 3)
    o_ref[...] = tn(perm_ref[...], held[...]).astype(BF16)
    sum_ref[...] = lax.dot_general(
        mine_ref[:, : by_unit.shape[0]], by_unit[...], (((1,), (0,)), ((), ())), precision=HIGH,
        preferred_element_type=F32,
    )
    routes.finish()


def finish_body(
    shards, chips, fc_ref, ada_ref, go_ref, gq_ref, one_ref, two_ref, gate_ref, cond_ref, tot_ref, gqa_ref,
    dm_ref, dc_ref, mine, up, inner_in, result, other, gq_all, sum_own, sum_pair, small, mods, conds, ada_s,
    local, sent, got,
):
    f, b = lax.axis_index("fsdp"), lax.axis_index("blk")
    z, c = b // 2, b % 2
    pair = b + 1 - 2 * c
    count = mine.shape[0]
    slots, wider = sum_own.shape
    size = wider // 6
    routes = Routes(sent, got)
    loads = fetch([(fc_ref, mine.at[0 : count - 1]), (ada_ref, ada_s)], local)
    greet(shards, chips)

    sum_own[:, 0 : 2 * size] = one_ref[...]
    sum_own[:, 2 * size : 3 * size] = gate_ref[:, 0:size]
    sum_own[:, 3 * size : 5 * size] = two_ref[...]
    sum_own[:, 5 * size : 6 * size] = gate_ref[:, size : 2 * size]
    routes.start("sum", sum_own, sum_pair, {"blk": pair})
    gq_all[b] = gq_ref[...]

    def line(side, s, send):
        away = s - 1 if send else s
        chip = z - away if side == 0 else z + away
        ahead = z + 1 < chips if side == 0 else z > 0
        known = z >= away if side == 0 else z + away < chips
        return chip, {"blk": b + 2 if side == 0 else b - 2}, known & ahead if send else known

    def send(name, s, place):
        for side in range(2):
            chip, to, when = line(side, s, True)
            routes.start((name, side, s), place(chip), place(chip), to, when)

    def take(name, s, place):
        for side in range(2):
            chip, _, when = line(side, s, False)
            routes.arrive((name, side, s), place(chip), when)
        if s + 1 < chips:
            send(name, s + 1, place)

    def head(chip):
        return gq_all.at[chip * 2 + c]

    send("head", 1, head)
    routes.start("head pair", gq_all.at[b], gq_all.at[b], {"blk": pair})

    half = chips // 2
    right = z // half
    inner, outer = {"blk": b + 2 - 4 * right}, {"blk": b - 2 + 4 * right}
    ends = (z > 0) & (z < chips - 1)
    middle = (z == half - 1) | (z == half)
    edge = jnp.logical_not(middle)

    parts = [[small.at[i] for i in range(4)]]
    parts += [[ref.at[i] for ref in (mine, up, inner_in, result)] for i in range(count)]
    count += 1

    def inward(i, when):
        own, above, within, _ = parts[i]
        routes.start(("up", i), own, above, inner, when & edge)
        routes.start(("across", i), own, within, inner, when & middle, ("in", i))

    mine[count - 2] = go_ref[...]
    routes.arrive("sum", sum_pair)
    total = sum_own[...] + sum_pair[...]
    small[0] = jnp.concatenate(
        [total[:, : 3 * size], total[:, 3 * size :]], axis=0
    ).astype(BF16)
    ahead = min(4, count)
    inward(0, jnp.logical_not(ends))
    loads[0].wait()
    for i in range(1, ahead):
        inward(i, jnp.logical_not(ends))

    def combine():
        mods[f, :, : 3 * size] = small[3, 0:slots].astype(F32)
        mods[f, :, 3 * size :] = small[3, slots : 2 * slots].astype(F32)
        for k in range(1, shards):
            routes.start(("mod", k), mods.at[f], mods.at[f], {"fsdp": flip(f, k)})

    def condition():
        for k in range(1, shards):
            routes.arrive(("mod", k), mods.at[flip(f, k)])
        dm_ref[...] = mods[...]
        loads[1].wait()
        grad = nt(mods[...].reshape(shards * slots, wider).astype(BF16), ada_s[...])
        values = cond_ref[...]
        gate = 1.0 / (1.0 + jnp.exp(-values))
        conds[f] = grad * (gate + values * gate * (1.0 - gate))
        for k in range(1, shards):
            routes.start(("cond", k), conds.at[f], conds.at[f], {"fsdp": flip(f, k)})

    def conditions():
        for k in range(1, shards):
            routes.arrive(("cond", k), conds.at[flip(f, k)])
        dc_ref[...] = conds[...]

    jobs = [combine, condition, conditions]
    heads = [lambda s=s: take("head", s, head) for s in range(1, chips)]

    def forward(i):
        own, above, _, _ = parts[i]
        routes.arrive(("up", i), above, ends)

        @pl.when(ends)
        def _():
            own[...] = (own[...].astype(F32) + above[...].astype(F32)).astype(BF16)

        inward(i, ends)
        if i + ahead < count:
            inward(i + ahead, jnp.logical_not(ends))

    def back(i):
        own, _, within, full = parts[i]
        routes.arrive(("in", i), within)

        @pl.when(middle)
        def _():
            full[...] = (own[...].astype(F32) + within[...].astype(F32)).astype(BF16)

        @pl.when(edge)
        def _():
            full[...] = within[...]

        routes.start(("down", i), full, within, outer, ends, ("in", i))
        if i:
            routes.start(("pair", i - 1), full, other.at[i - 1], {"blk": pair})

    for i in range(count + 1):
        if i < count:
            forward(i)
        if i:
            back(i - 1)
            if jobs and i % 2 == 1:
                jobs.pop(0)()
            if heads and i % 2 == 0 and i > 2:
                heads.pop(0)()
    for job in jobs + heads:
        job()
    for s in range(1, chips):
        for side in range(2):
            chip, _, when = line(side, s, False)
            routes.start(("head pair", side, s), head(chip), head(chip), {"blk": pair}, when)
    copies = fetch([(result, tot_ref.at[c])], local)
    for i in range(count - 1):
        routes.arrive(("pair", i), other.at[i])
    copies += fetch([(other, tot_ref.at[1 - c])], local, 1)
    routes.arrive("head pair", gq_all.at[pair])
    for s in range(1, chips):
        for side in range(2):
            chip, _, when = line(side, s, False)
            routes.arrive(("head pair", side, s), gq_all.at[chip * 2 + 1 - c], when)
    copies += fetch([(gq_all, gqa_ref)], local, 2)
    routes.finish()
    for copy in copies:
        copy.wait()


def unfold_body(
    shards, low_ref, wave_ref, dm_ref, dc_ref, tot_ref, gq_ref, temb_ref, ada_ref, qkv_ref, out_ref,
    fc1_ref, fc2_ref, tot_s, gq_s, ada_s, qkv_s, out_s, fc1_s, fc2_s, loads, sems,
):
    _, count, rows, size = tot_ref.shape
    slots = dm_ref.shape[1]
    inside = fetch([(tot_ref, tot_s), (gq_ref, gq_s)], loads)
    copies = []

    def leave(source, target):
        copy = pltpu.make_async_copy(source, target, sems.at[len(copies)])
        copy.start()
        copies.append(copy)

    grads = dm_ref[...].reshape(shards * slots, -1).astype(BF16)
    ada_s[...] = tn(low_ref[...], grads)
    leave(ada_s, ada_ref)
    inside[0].wait()
    hidden = fc1_s.shape[1]
    part = hidden // shards // 2
    height = fc1_s.shape[0]
    blocks = hidden // 2 // size
    per = height // rows
    for core in range(2):
        for i in range(blocks * per):
            piece = tot_s[core, i].astype(F32)
            block, at = i // per, (i % per) * rows
            for j in range(size // part):
                column = (block * (size // part) + j) * 2 * part + core * part
                fc1_s[at : at + rows, column : column + part] = piece[:, j * part : (j + 1) * part]
        rest = count - 1 - blocks * per
        for i in range(rest):
            at = (core * rest + i) * rows
            fc2_s[at : at + rows, :] = tot_s[core, blocks * per + i].astype(F32)
        out_s[core * rows : (core + 1) * rows, :] = tot_s[core, count - 1].astype(F32)
    leave(fc1_s, fc1_ref)
    leave(fc2_s, fc2_ref)
    leave(out_s, out_ref)
    inside[1].wait()
    devices, _, packed = gq_ref.shape
    narrow = packed // 3
    for p in range(3):
        for i in range(devices):
            at = p * size + i * narrow
            qkv_s[:, at : at + narrow] = gq_s[i, :, p * narrow : (p + 1) * narrow].astype(F32)
    leave(qkv_s, qkv_ref)
    step = dc_ref.shape[2]
    for i in range(shards):
        temb_ref[:, i * step : (i + 1) * step] = lax.dot_general(
            wave_ref[...], dc_ref[i], (((0,), (0,)), ((), ())), precision=HIGH,
            preferred_element_type=F32,
        )
    for copy in copies:
        copy.wait()


def on_device(
    tokens,
    timesteps,
    segment_ids,
    head_mask,
    chan_mask,
    token_mask,
    w_temb,
    w_ada,
    w_qkv,
    w_out,
    w_fc1,
    w_fc2,
    cotangent,
):
    count, size = tokens.shape
    slots, heads = head_mask.shape[1:]
    head_size = size // heads
    shards, blocks = lax.axis_size("fsdp"), lax.axis_size("blk")
    chips = blocks // 2
    f, b = lax.axis_index("fsdp"), lax.axis_index("blk")
    c = b % 2
    width = BLOCK // blocks
    units = count // width
    own = heads // blocks
    wide = 3 * own * LANES
    hidden = w_fc1.shape[1]
    half = hidden // 2
    ids = jnp.stack([f, b, c]).astype(I32)

    near = 3 if shards == 4 else shards
    row1, row2 = w_fc1.shape[0], w_fc2.shape[0] // 2
    fc_blocks = half // size
    fc_rows = fc_blocks * row1 + row2

    items = lax.dynamic_slice_in_dim(segment_ids, b * count, count, axis=1)
    rows = w_temb.shape[0]
    entries = rows * shards
    spectrum = frequencies(timesteps[0], entries).astype(BF16).astype(F32)
    out_rows = w_out.shape[0] // 2
    ada_rows, wider = w_ada.shape
    padded = -(-units // 8) * 8
    n_copies = 9 * shards + 4 * chips + 12
    outs = run(
        "front",
        functools.partial(front_body, shards, chips, heads),
        [
            (VMEM, a)
            for a in (items, token_mask[None, :], tokens, cotangent, spectrum, w_temb)
        ]
        + [(ANY, a) for a in (w_ada, w_qkv, w_out.reshape(2, out_rows, size), w_fc1, w_fc2)],
        [
            (VMEM, shape((count, size))),
            (VMEM, shape((count, size))),
            (ANY, shape((2, slots, count), F32)),
            (VMEM, shape((8, LANES), I32)),
            (VMEM, shape((slots, LANES), F32)),
            (VMEM, shape((count, count))),
            (VMEM, shape((padded, wider), F32)),
            (VMEM, shape((shards * slots, ada_rows), F32)),
            (VMEM, shape((shards * slots, ada_rows))),
            (VMEM, shape((shards * slots, rows), F32)),
            (ANY, shape((2, count, size))),
            (ANY, shape((units, BLOCK, size))),
            (VMEM, shape((units, BLOCK, wide))),
            (VMEM, shape((size, wide))),
            (ANY, shape((shards, 2, out_rows, size))),
            (ANY, shape((row2, size))),
        ]
        + [(ANY, shape((fc_blocks, row1, size)))] * near,
        [
            pltpu.VMEM((blocks, count, size), BF16),
            pltpu.VMEM((shards, slots, entries), F32),
            pltpu.VMEM((shards, rows, size), BF16),
            pltpu.VMEM((shards, 2, slots, wider // 2), F32),
            pltpu.VMEM((shards, slots, wider // 2), F32),
            pltpu.VMEM((2, slots, wider // 2), F32),
            pltpu.VMEM((2, slots, count), F32),
            pltpu.VMEM((2, count, size), BF16),
            pltpu.VMEM((shards, w_qkv.shape[0], 3 * own * head_size), BF16),
            pltpu.VMEM((shards, 2, out_rows, size), BF16),
            pltpu.VMEM((count, size), BF16),
            pltpu.VMEM(w_ada.shape, BF16),
            pltpu.VMEM(w_qkv.shape, BF16),
            pltpu.VMEM(w_fc1.shape, BF16),
            pltpu.VMEM((near, fc_blocks, row1, size), BF16),
            pltpu.SemaphoreType.DMA((units + 4 + near,)),
            pltpu.SemaphoreType.DMA((5,)),
            pltpu.SemaphoreType.DMA((n_copies,)),
            pltpu.SemaphoreType.DMA((n_copies,)),
        ],
        flops=2 * units * BLOCK * size * wide,
        collective=0,
    )
    x_s, c_s, hots, info, mark, perm, mod, condition, lifted, waves, dms = outs[:11]
    normed, qkv, w_heads, w_out_all, fc2_own = outs[11:16]
    fc1_near = outs[16:]
    fc1_parts = [(a, k, 0) for k, a in enumerate(fc1_near)]
    if shards == 4 and fc_blocks == 2:
        one, two = swap(fc2_own, "fsdp", 1), swap(fc2_own, "fsdp", 2)
        cut = row2 // 2
        fc2_parts = [(fc2_own, 0, 0), (one, 1, 0), (two, 2, 0)]
        moves = [
            (fc1_near[1], (0, 1, 2)),
            (fc1_near[2], (1, 2, 1)),
            (one, (0, cut, 2)),
            (two, (cut, row2, 1)),
        ]
    else:
        fc1_parts += [
            (swap(fc1_near[0], "fsdp", k), k, 0) for k in range(len(fc1_near), shards)
        ]
        moves = []
        fc2_parts = [(fc2_own, 0, 0)] + [(swap(fc2_own, "fsdp", k), k, 0) for k in range(1, shards)]
    w_out_all = w_out_all.reshape(size, size)

    mask = head_mask[0]
    narrow = own * head_size
    held, lse, pieces = run(
        "attend",
        functools.partial(attend_body, own, head_size, blocks),
        [(SMEM, ids), (SMEM, info), (SMEM, mask), (VMEM, qkv)],
        [
            (VMEM, shape((units, narrow, BLOCK))),
            (VMEM, shape((units, 8, BLOCK), F32)),
            (VMEM, shape((blocks, narrow, count))),
        ],
        [
            pltpu.VMEM((units, narrow, BLOCK), F32),
            pltpu.VMEM((units, own, -(-head_size // 16) * 16, BLOCK), BF16),
            pltpu.VMEM((blocks, narrow, count), BF16),
        ],
        flops=2 * units * units * BLOCK * BLOCK * wide // 3,
    )
    if moves:
        moved = lax.optimization_barrier(tuple(a for a, _ in moves) + (lse,))[:-1]
    else:
        moved = ()
    plan = [move for _, move in moves]
    n_copies = blocks + len(moves) + 1
    outs = run(
        "project",
        functools.partial(project_body, shards, blocks, plan),
        [(VMEM, a) for a in (mod, x_s, w_out_all, pieces)] + [(ANY, a) for a in moved],
        [
            (VMEM, shape((count, size), F32)),
            (VMEM, shape((count, size), F32)),
            (ANY, shape((2, count, size))),
            (VMEM, shape((size, count))),
        ]
        + [(ANY, shape((high - low,) + a.shape[1:])) for a, (low, high, _) in moves],
        [
            pltpu.VMEM((blocks, narrow, count), BF16),
            pltpu.VMEM((2, count, size), BF16),
            pltpu.SemaphoreType.DMA((1,)),
            pltpu.SemaphoreType.DMA((n_copies,)),
            pltpu.SemaphoreType.DMA((n_copies,)),
        ],
        flops=2 * count * size * size,
        collective=3,
    )
    attn, x1, h2, om = outs[:4]
    if moves:
        fc1_parts += [(outs[4], 3, 0), (outs[5], 3, 1)]
        fc2_parts += [(outs[6], 3, 0), (outs[7], 3, cut)]

    chan = chan_mask[0].reshape(slots, shards, 2, half // shards)
    chan = lax.dynamic_slice_in_dim(chan, c, 1, axis=2).reshape(slots, half)
    ff_step = 768
    n_sems = 4 + 4 * shards * (half // ff_step + 1)
    mlp, mlp_send, dh2, dh2_send, g_fc = run(
        "feed_forward",
        functools.partial(
            ff_body,
            shards,
            ff_step,
            2,
            [(k, first) for _, k, first in fc1_parts],
            [(k, first) for _, k, first in fc2_parts],
        ),
        [(SMEM, ids), (VMEM, hots), (VMEM, chan)]
        + [(ANY, a) for a in (h2, dms)]
        + [(ANY, a) for a, _, _ in fc1_parts + fc2_parts],
        [
            (VMEM, shape((count, size), F32)),
            (VMEM, shape((count, size))),
            (VMEM, shape((count, size), F32)),
            (VMEM, shape((count, size))),
            (ANY, shape((shards, fc_rows, size))),
        ],
        [
            pltpu.VMEM((size, half), BF16),
            pltpu.VMEM((half, size), BF16),
            pltpu.VMEM((2 * count, size), BF16),
            pltpu.VMEM((2 * count, size), BF16),
            pltpu.VMEM((size, 2 * count), BF16),
            pltpu.VMEM((2 * count, ff_step), BF16),
            pltpu.VMEM((2 * count, ff_step), BF16),
            pltpu.VMEM((2 * count, size), F32),
            pltpu.VMEM((2 * count, size), F32),
            pltpu.VMEM((size, half), BF16),
            pltpu.VMEM((half, size), BF16),
            pltpu.SemaphoreType.DMA((n_sems,)),
        ],
        flops=6 * 2 * 2 * count * size * half,
    )
    g_fc = lax.psum_scatter(
        g_fc.reshape(shards * fc_rows, size), "fsdp", scatter_dimension=0, tiled=True
    )

    n_copies = blocks + 2
    up_parts, dx1, sums_two, sums_gate, result, g_out, g_out_send = run(
        "middle_back",
        functools.partial(middle_body, shards, blocks),
        [(VMEM, a) for a in (mod, mark, x1, c_s, dh2)]
        + [(ANY, a) for a in (dh2_send, mlp, mlp_send, attn, om)]
        + [(ANY, w_out_all.reshape(blocks, narrow, size)), (VMEM, perm)],
        [
            (VMEM, shape((blocks, narrow, count))),
            (VMEM, shape((count, size), F32)),
            (VMEM, shape((slots, 2 * size), F32)),
            (VMEM, shape((slots, 2 * size), F32)),
            (VMEM, shape((count, size))),
            (VMEM, shape((shards, out_rows, size))),
            (VMEM, shape((shards, out_rows, size))),
        ],
        [
            pltpu.VMEM((count, size), BF16),
            pltpu.VMEM((count, size), BF16),
            pltpu.VMEM((count, size), BF16),
            pltpu.VMEM((blocks, narrow, count), BF16),
            pltpu.VMEM((blocks, narrow, count), BF16),
            pltpu.VMEM((count, size), BF16),
            pltpu.VMEM((2 * shards, out_rows, size), BF16),
            pltpu.VMEM((padded, 2 * size), F32),
            pltpu.VMEM((blocks, narrow, size), BF16),
            pltpu.VMEM((count, size), F32),
            pltpu.VMEM((count, size), F32),
            pltpu.VMEM((size, count), BF16),
            pltpu.SemaphoreType.DMA((4,)),
            pltpu.SemaphoreType.DMA((n_copies,)),
            pltpu.SemaphoreType.DMA((n_copies,)),
        ],
        flops=4 * count * size * size,
        collective=4,
    )

    (d_qkv,) = run(
        "attend_back",
        functools.partial(attend_back_body, own, head_size, blocks),
        [(SMEM, ids), (SMEM, info), (SMEM, mask)]
        + [(VMEM, a) for a in (qkv, held, lse, up_parts)],
        [(VMEM, shape((units, BLOCK, wide)))],
        [
            pltpu.VMEM((units, own, LANES, BLOCK), BF16),
            pltpu.VMEM((units, 8, BLOCK), F32),
            pltpu.VMEM((units, own, LANES, BLOCK), F32),
            pltpu.VMEM((own, BLOCK, LANES), F32),
            pltpu.VMEM((own, BLOCK, LANES), F32),
        ],
        flops=5 * units * units * BLOCK * BLOCK * wide // 3,
    )
    per = 4 if units % 4 == 0 else 1
    rows_qkv = w_qkv.shape[0]
    n_copies = 4 * chips + 2 * shards + 4
    grad_tokens, sums_one, g_qkv, g_out = run(
        "stream_back",
        functools.partial(stream_back_body, shards, chips, heads, per),
        [(ANY, normed), (ANY, g_out_send)]
        + [(VMEM, a) for a in (d_qkv, w_heads, mod, mark, x_s, dx1, perm, g_out)],
        [
            (VMEM, shape((count, size))),
            (VMEM, shape((slots, 2 * size), F32)),
            (VMEM, shape((rows_qkv, 3 * narrow))),
            (VMEM, shape((out_rows, size))),
        ],
        [
            pltpu.VMEM((chips, count, size), BF16),
            pltpu.VMEM((chips, count, size), BF16),
            pltpu.VMEM((chips, count, size), BF16),
            pltpu.VMEM((chips + 1, count, size), BF16),
            pltpu.VMEM((2, per, BLOCK, size), BF16),
            pltpu.VMEM((size, wide), F32),
            pltpu.VMEM((shards, rows_qkv, 3 * narrow), BF16),
            pltpu.VMEM((shards, rows_qkv, 3 * narrow), BF16),
            pltpu.VMEM((shards, out_rows, size), BF16),
            pltpu.VMEM((shards, out_rows, size), BF16),
            pltpu.VMEM((shards, out_rows, size), BF16),
            pltpu.VMEM((count, size), F32),
            pltpu.VMEM((count, size), BF16),
            pltpu.VMEM((padded, 2 * size), F32),
            pltpu.SemaphoreType.DMA((2,)),
            pltpu.SemaphoreType.DMA((n_copies,)),
            pltpu.SemaphoreType.DMA((n_copies,)),
        ],
        flops=4 * units * BLOCK * size * wide,
        collective=1,
    )

    pieces = fc_rows // out_rows
    n_copies = 5 * pieces + 16 + 4 * chips + 2 * shards
    totals, g_qkv, d_mod, d_cond = run(
        "finish",
        functools.partial(finish_body, shards, chips),
        [(ANY, g_fc.reshape(pieces, out_rows, size)), (ANY, w_ada)]
        + [(VMEM, a) for a in (g_out, g_qkv, sums_one, sums_two, sums_gate, condition)],
        [
            (ANY, shape((2, pieces + 1, out_rows, size))),
            (ANY, shape((blocks, rows_qkv, 3 * narrow))),
            (VMEM, shape((shards, slots, wider), F32)),
            (VMEM, shape((shards, shards * slots, ada_rows), F32)),
        ],
        [pltpu.VMEM((pieces + 1, out_rows, size), BF16)] * 5
        + [
            pltpu.VMEM((blocks, rows_qkv, 3 * narrow), BF16),
            pltpu.VMEM((slots, wider), F32),
            pltpu.VMEM((slots, wider), F32),
            pltpu.VMEM((4, 2 * slots, wider // 2), BF16),
            pltpu.VMEM((shards, slots, wider), F32),
            pltpu.VMEM((shards, shards * slots, ada_rows), F32),
            pltpu.VMEM(w_ada.shape, BF16),
            pltpu.SemaphoreType.DMA((3,)),
            pltpu.SemaphoreType.DMA((n_copies,)),
            pltpu.SemaphoreType.DMA((n_copies,)),
        ],
        collective=2,
    )
    grad_temb, grad_ada, grad_qkv, grad_out, grad_fc1, grad_fc2 = run(
        "unfold",
        functools.partial(unfold_body, shards),
        [(VMEM, a) for a in (lifted, waves, d_mod, d_cond)] + [(ANY, totals), (ANY, g_qkv)],
        [
            (VMEM, shape(w_temb.shape, F32)),
            (ANY, shape(w_ada.shape, F32)),
            (ANY, shape(w_qkv.shape, F32)),
            (ANY, shape(w_out.shape, F32)),
            (ANY, shape(w_fc1.shape, F32)),
            (ANY, shape(w_fc2.shape, F32)),
        ],
        [pltpu.VMEM(a.shape, BF16) for a in (totals, g_qkv)]
        + [pltpu.VMEM(a.shape, F32) for a in (w_ada, w_qkv, w_out, w_fc1, w_fc2)]
        + [pltpu.SemaphoreType.DMA((2,)), pltpu.SemaphoreType.DMA((5,))],
    )
    return (
        result,
        grad_tokens,
        grad_temb,
        grad_ada,
        grad_qkv,
        grad_out,
        grad_fc1,
        grad_fc2,
    )


def solution(mesh):
    placed = (
        P(("fsdp", "blk"), None),
        P("fsdp", None),
        P("fsdp", None),
        P("fsdp", None, None),
        P("fsdp", None, None),
        P(("fsdp", "blk")),
        P("fsdp", None),
        P("fsdp", None),
        P("fsdp", None),
        P("fsdp", None),
        P("fsdp", None),
        P("fsdp", None),
        P(("fsdp", "blk"), None),
    )
    return jax.shard_map(
        on_device,
        mesh=mesh,
        in_specs=placed,
        out_specs=(
            P(("fsdp", "blk"), None),
            P(("fsdp", "blk"), None),
            P("fsdp", None),
            P("fsdp", None),
            P("fsdp", None),
            P("fsdp", None),
            P("fsdp", None),
            P("fsdp", None),
        ),
        check_vma=False,
    )
```

profile of v0, /device:TPU:1, one launch (start us, length us, event | category | flops | bytes accessed | tf_op | source)
XLA Modules:
  0.0 479.6 jit_solution(3211285972310064589)
XLA Ops:
  7.2 0.0 copy-start
  7.2 0.0 reduce-scatter.2.cloned.1.call-start
  7.2 0.7 convert_bitcast_fusion
  7.9 1.2 broadcast_in_dim.2.keep_ref
  9.2 0.6 constant_dynamic-slice_fusion.items_ref
  9.7 0.1 fusion
  9.8 0.6 maximum_convert_fusion.spec_ref
  10.4 81.4 %front.1 = (bf16[384,1152]{1,0:T(8,128)(2,1)}, bf16[384,1152]{1,0:T(8,128)(2,1)}, f32[2,8,384]{2,1,0:T(8,128)}, s32[8,128]{1,0:T(8,128)}, f32[8,128]{1,0:T(8,128...) custom-call(s32[1,384]{1,0:T(1,128)} %constant_dynamic-slice_fusion., ...), custom_call_target="tpu_custom_call" | custom-call | flops 5435817984 | bytes 39773184 | tf_op jit(solution)/shard_map/front/pallas_call | solution.py:32
  91.9 0.3 collective-permute-start.1
  92.2 1.7 collective-permute-start
  93.9 0.2 reshape_squeeze.3
  94.1 0.3 dynamic-slice_reduce_fusion
  94.4 0.7 reshape.45.chan_ref
  95.1 0.6 pad_add_fusion.ids_ref
  95.7 21.3 %attend.1 = (bf16[12,144,256]{2,1,0:T(8,128)(2,1)}, f32[12,8,256]{2,1,0:T(8,128)}, bf16[8,144,384]{2,1,0:T(8,128)(2,1)}) custom-call(s32[3]{0:T(128)} %pad_add_fusion.ids_ref, s32[8,128]{1,0:T(8,128)} %get-tuple-element.72.info_ref, s32[8,16]{1,0:T(8,128)} %bitcast.16, bf16[12,256,768]{2,1,0:T(8,128)(2,1)} %get-tuple-element.73.qkv_ref), custom_call_target="tpu_custom_call" | custom-call | flops 4831838208 | bytes 6590988 | tf_op jit(solution)/shard_map/attend/pallas_call | solution.py:32
  117.0 3.9 collective-permute-done.1.refs_3_.refs_7_
  120.9 0.4 collective-permute-done.refs_2_.refs_6_
  121.3 0.6 copy-done.2
  121.9 39.6 %project.1 = (f32[384,1152]{1,0:T(8,128)}, f32[384,1152]{1,0:T(8,128)}, bf16[2,384,1152]{2,1,0:T(8,128)(2,1)}, bf16[1152,384]{1,0:T(8,128)(2,1)}, bf16[1,288,115...) custom-call(f32[16,6912]{1,0:T(8,128)} %get-tuple-element.68.mod_ref, ...), custom_call_target="tpu_custom_call" | custom-call | flops 1019215872 | bytes 19021824 | tf_op jit(solution)/shard_map/project/pallas_call | solution.py:32
  161.5 39.0 %feed_forward.1 = (f32[384,1152]{1,0:T(8,128)}, bf16[384,1152]{1,0:T(8,128)(2,1)}, f32[384,1152]{1,0:T(8,128)}, bf16[384,1152]{1,0:T(8,128)(2,1)}, bf16[4,1152,1152]{2,1,0:T(8,128)(2,1)}) custom-call(s32[3]{0:T(128)} %pad_add_fusion.ids_ref, f32[2,8,384]{2,1,0:T(8,128)} %get-tuple-element.85.hot_ref, s32[8,2304]{1,0:T(8,128)} %reshape.45.chan_ref, ...), custom_call_target="tpu_custom_call" | custom-call | flops 24461180928 | bytes 30179340 | tf_op jit(solution)/shard_map/feed_forward/pallas_call | solution.py:32
  200.5 0.0 reduce-scatter.2.cloned.1.call-update
  200.5 33.4 %middle_back.1 = (bf16[8,144,384]{2,1,0:T(8,128)(2,1)}, f32[384,1152]{1,0:T(8,128)}, f32[8,2304]{1,0:T(8,128)}, f32[8,2304]{1,0:T(8,128)}, bf16[384,1152]{1,0:T(...) custom-call(f32[16,6912]{1,0:T(8,128)} %get-tuple-element.68.mod_ref, ...), custom_call_target="tpu_custom_call" | custom-call | flops 2038431744 | bytes 20353024 | tf_op jit(solution)/shard_map/middle_back/pallas_call | solution.py:32
  233.9 30.8 %attend_back.1.d_ref = bf16[12,256,768]{2,1,0:T(8,128)(2,1)} custom-call(s32[3]{0:T(128)} %pad_add_fusion.ids_ref, s32[8,128]{1,0:T(8,128)} %get-tuple-element.72.info_ref, s32[8,16]{1,0:T(8,128)} %bitcast.17, bf16[12,256,768]{2,1,0:T(8,128)(2,1)} %get-tuple-element.73.qkv_ref, bf16[12,144,256]{2,1,0:T(8,128)(2,1)} %get-tuple-element.103.o_ref, ...), custom_call_target="tpu_custom_call" | custom-call | flops 12079595520 | bytes 11309580 | tf_op jit(solution)/shard_map/attend_back/pallas_call | solution.py:32
  264.8 78.8 %stream_back.1 = (bf16[384,1152]{1,0:T(8,128)(2,1)}, f32[8,2304]{1,0:T(8,128)}, bf16[288,432]{1,0:T(8,128)(2,1)}, bf16[144,1152]{1,0:T(8,128)(2,1)}) custom-call(bf16[12,256,1152]{2,1,0:T(8,128)(2,1)} %get-tuple-element.101.h_ref, bf16[4,144,1152]{2,1,0:T(8,128)(2,1)} %get-tuple-element.102.gs_ref, bf16[12,256,768]{2,1,0:T(8,128)(2,1)} %attend_back.1.d_ref, ...), custom_call_target="tpu_custom_call" | custom-call | flops 10871635968 | bytes 21154816 | tf_op jit(solution)/shard_map/stream_back/pallas_call | solution.py:32
  343.6 0.0 reduce-scatter.2.cloned.1.call-done
  343.6 114.3 %finish.1 = (bf16[2,9,144,1152]{3,2,1,0:T(8,128)(2,1)}, bf16[8,288,432]{2,1,0:T(8,128)(2,1)}, f32[4,8,6912]{2,1,0:T(8,128)}, f32[4,32,288]{2,1,0:T(8,128)}) custom-call(bf16[8,144,1152]{2,1,0:T(8,128)(2,1)} %bitcast.14, bf16[288,6912]{1,0:T(8,128)(2,1)} %ada_ref.3, bf16[144,1152]{1,0:T(8,128)(2,1)} %get-tuple-element.112.go_ref, ...), custom_call_target="tpu_custom_call" | custom-call | bytes 16468992 | tf_op jit(solution)/shard_map/finish/pallas_call | solution.py:32
  457.9 0.0 copy-start.3
  457.9 12.2 %unfold.1 = (f32[64,1152]{1,0:T(8,128)}, f32[288,6912]{1,0:T(8,128)}, f32[288,3456]{1,0:T(8,128)}, f32[288,1152]{1,0:T(8,128)}, f32[288,4608]{1,0:T(8,128)}, /*index=5*/f32[1152,1152]{1,0:T(8,128)}) custom-call(bf16[32,288]{1,0:T(8,128)(2,1)} %get-tuple-element.109.low_ref, f32[32,64]{1,0:T(8,128)} %get-tuple-element.110.wave_ref, ...), custom_call_target="tpu_custom_call" | custom-call | bytes 33204224 | tf_op jit(solution)/shard_map/unfold/pallas_call | solution.py:32
  470.1 0.0 copy-start.1
  470.1 0.9 copy.25
  471.0 0.5 copy-done.4
  471.5 0.9 copy.26
  (8 shorter events, 0.0 us)
Async XLA Ops:
  7.2 2.0 copy-start
  7.2 336.4 %reduce-scatter.2.cloned.1.call-start = ((), (), s32[]{:S(2)}) async-start(), calls=%async_computation.1 | async-start | bytes 13271040 | tf_op jit(solution)/shard_map/reduce_scatter | solution.py:1459
  10.4 83.5 %copy-start.5 = (s32[1,8,4608]{2,1,0:T(8,128)S(1)}, s32[1,8,4608]{2,1,0:T(8,128)}, u32[]{:S(2)}) copy-start(s32[1,8,4608]{2,1,0:T(8,128)} %param.17) | copy-start | bytes 442372
  91.9 29.0 %collective-permute-start.1 = (bf16[576,1152]{1,0:T(8,128)(2,1)}, bf16[576,1152]{1,0:T(8,128)(2,1)S(1)}, u32[]{:S(2)}, u32[]{:S(2)}) collective-permute-start(bf16[576,1152]{1,0:T(8,128)(2,1)} %get-tuple-element.77.refs_5_), channel_id=1, source_target_pairs={{0,16},{8,24},{16,0},{24,8},{1,17},{9,25},{17,1},{25,9},{2,18},{10... | collective-permute-start | bytes 3981320 | tf_op jit(solution)/shard_map/ppermute | solution.py:51
  92.2 29.1 %collective-permute-start = (bf16[576,1152]{1,0:T(8,128)(2,1)}, bf16[576,1152]{1,0:T(8,128)(2,1)}, u32[]{:S(2)}, u32[]{:S(2)}) collective-permute-start(bf16[576,1152]{1,0:T(8,128)(2,1)} %get-tuple-element.77.refs_5_), channel_id=1, source_target_pairs={{0,8},{8,0},{16,24},{24,16},{1,9},{9,1},{17,25},{25,17},{2,10},{10... | collective-permute-start | bytes 3981320 | tf_op jit(solution)/shard_map/ppermute | solution.py:51
  120.9 1.1 copy-start.2
  457.9 12.2 %copy-start.3 = (bf16[384,1152]{1,0:T(8,128)(2,1)S(1)}, bf16[384,1152]{1,0:T(8,128)(2,1)}, u32[]{:S(2)}) copy-start(bf16[384,1152]{1,0:T(8,128)(2,1)} %get-tuple-element.138) | copy-start | bytes 2654212
  470.1 1.5 copy-start.4
  470.1 2.4 copy-start.1
Sparse Core Ops, SparseCore 0:
  200.6 123.8 reduce-scatter.1
where the time goes:
time: 484 us; the launch traced here: 480 us
  Pallas kernels  451 us (93%)
  between operations  14.4 us (3%)
  local copies, waits for them, and re-layouts  5.98 us (1%)
    pallas_call x9, Pallas kernels, run(): pl.pallas_call(body, out_shape=[o for _, o in outs], in_specs=[s for s, _...  451 us
  transfers between devices with their start and end apart: 3, of which 2 were waited for; matrix products, arithmetic and copies ran while one was open for 0% of the time, Pallas kernels for 34%

commit v1 on v0

--- a/solution.py
+++ b/solution.py
@@ -455,22 +455,19 @@
         routes.arrive(("out", 3, 1), wo_all.at[other, c, :, 0:cut])
         routes.arrive(("out", 3, 2), wo_all.at[other, c, :, cut:size])
         routes.start(("pair out", 3), wo_all.at[other, c], wo_all.at[other, c], {"blk": pair})
-    work(chips - 1)
     inside[2].wait()
-    for k in range(1, len(fc_refs)):
-        routes.arrive(("fc", k), fc_all.at[k])
-    inside[4].wait()
     for k in range(1, shards):
         routes.arrive(("pair out", k), wo_all.at[flip(f, k), 1 - c])
     routes.arrive("dm", dms.at[1])
     routes.arrive("hot", hots.at[1])
+    done = fetch([(wo_all, wo_ref), (dms, dm_ref), (hots, hot_ref)], local, units)
+    work(chips - 1)
+    for k in range(1, len(fc_refs)):
+        routes.arrive(("fc", k), fc_all.at[k])
+    inside[4].wait()
+    done += fetch([(fc_all.at[k], ref) for k, ref in enumerate(fc_refs)], local, units + 3)
     routes.finish()
-    copies = fetch(
-        [(wo_all, wo_ref), (dms, dm_ref), (hots, hot_ref)]
-        + [(fc_all.at[k], ref) for k, ref in enumerate(fc_refs)],
-        local,
-    )
-    for copy in copies:
+    for copy in done:
         copy.wait()
 
 
@@ -878,7 +875,7 @@
 def stream_back_body(
     shards, chips, heads, per, h_ref, gs_ref, d_ref, wh_ref, mod_ref, mine_ref, x_ref, dx_ref, perm_ref,
     gm_ref, o_ref, sum_ref, g_ref, go_ref, give, take, keep, came, h_s, acc, low, others, out_in, out_low,
-    out_got, total, held, by_unit, local, sent, got,
+    out_got, total, held, x_s, dx_s, perm_s, late, by_unit, local, sent, got,
 ):
     f, b = lax.axis_index("fsdp"), lax.axis_index("blk")
     z, c = b // 2, b % 2
@@ -899,6 +896,7 @@
         )
 
     load(0).start()
+    loaded = fetch([(x_ref, x_s), (dx_ref, dx_s), (perm_ref, perm_s)], late)
     greet(shards, chips)
     routes.start("out", gs_ref, out_in, {"blk": pair})
 
@@ -1015,19 +1013,21 @@
                 total[...] += came[slot].astype(F32)
 
     by_unit[...] = jnp.zeros_like(by_unit)
+    for copy in loaded:
+        copy.wait()
 
     def one(u):
         rows = pl.ds(pl.multiple_of(u * width, width), width)
         scale = mod_ref[pl.ds(u, 1), size : 2 * size]
-        normed, spread = normal(x_ref[rows, :].astype(F32))
+        normed, spread = normal(x_s[rows, :].astype(F32))
         grad = total[rows, :]
         by_unit[pl.ds(u, 1), 0:size] = jnp.sum(grad, axis=0, keepdims=True)
         by_unit[pl.ds(u, 1), size : 2 * size] = jnp.sum(grad * normed, axis=0, keepdims=True)
-        dx = dx_ref[rows, :] + normal_back(grad * (1.0 + scale), normed, spread)
+        dx = dx_s[rows, :] + normal_back(grad * (1.0 + scale), normed, spread)
         held[rows, :] = dx.astype(BF16)
 
     each(units, one, 3)
-    o_ref[...] = tn(perm_ref[...], held[...]).astype(BF16)
+    o_ref[...] = tn(perm_s[...], held[...]).astype(BF16)
     sum_ref[...] = lax.dot_general(
         mine_ref[:, : by_unit.shape[0]], by_unit[...], (((1,), (0,)), ((), ())), precision=HIGH,
         preferred_element_type=F32,
@@ -1519,7 +1519,9 @@
         "stream_back",
         functools.partial(stream_back_body, shards, chips, heads, per),
         [(ANY, normed), (ANY, g_out_send)]
-        + [(VMEM, a) for a in (d_qkv, w_heads, mod, mark, x_s, dx1, perm, g_out)],
+        + [(VMEM, a) for a in (d_qkv, w_heads, mod, mark)]
+        + [(ANY, a) for a in (x_s, dx1, perm)]
+        + [(VMEM, g_out)],
         [
             (VMEM, shape((count, size))),
             (VMEM, shape((slots, 2 * size), F32)),
@@ -1540,6 +1542,10 @@
             pltpu.VMEM((shards, out_rows, size), BF16),
             pltpu.VMEM((count, size), F32),
             pltpu.VMEM((count, size), BF16),
+            pltpu.VMEM((count, size), BF16),
+            pltpu.VMEM((count, size), F32),
+            pltpu.VMEM((count, count), BF16),
+            pltpu.SemaphoreType.DMA((3,)),
             pltpu.VMEM((padded, 2 * size), F32),
             pltpu.SemaphoreType.DMA((2,)),
             pltpu.SemaphoreType.DMA((n_copies,)),

time: 484 us -> 486 us (level)
  no operation moved by 1% of the time
where the time goes in v1:
time: 486 us; the launch traced here: 483 us
  Pallas kernels  452 us (93%)
  between operations  14.4 us (3%)
  waiting for transfers between devices  6.68 us (1%)
  local copies, waits for them, and re-layouts  6.05 us (1%)
    pallas_call x9, Pallas kernels, run(): pl.pallas_call(body, out_shape=[o for _, o in outs], in_specs=[s for s, _...  452 us
  transfers between devices with their start and end apart: 3, of which 2 were waited for; matrix products, arithmetic and copies ran while one was open for 0% of the time, Pallas kernels for 34%

profile of v1, /device:TPU:1, one launch (start us, length us, event | category | flops | bytes accessed | tf_op | source)
XLA Modules:
  0.0 483.0 jit_solution(7532595677095317606)
XLA Ops:
  7.2 0.0 copy-start
  7.2 0.0 reduce-scatter.2.cloned.1.call-start
  7.2 0.7 convert_bitcast_fusion
  7.9 1.2 broadcast_in_dim.2.keep_ref
  9.2 0.0 copy-done
  9.2 0.6 constant_dynamic-slice_fusion.items_ref
  9.7 0.1 fusion
  9.8 0.6 maximum_convert_fusion.spec_ref
  10.4 83.4 %front.1 = (bf16[384,1152]{1,0:T(8,128)(2,1)}, bf16[384,1152]{1,0:T(8,128)(2,1)}, f32[2,8,384]{2,1,0:T(8,128)}, s32[8,128]{1,0:T(8,128)}, f32[8,128]{1,0:T(8,128...) custom-call(s32[1,384]{1,0:T(1,128)} %constant_dynamic-slice_fusion., ...), custom_call_target="tpu_custom_call" | custom-call | flops 5435817984 | bytes 39773184 | tf_op jit(solution)/shard_map/front/pallas_call | solution.py:32
  93.9 0.5 collective-permute-start.1
  94.3 1.6 collective-permute-start
  95.9 0.2 reshape_squeeze.3
  96.1 0.3 dynamic-slice_reduce_fusion
  96.3 0.7 reshape.45.chan_ref
  97.1 0.6 pad_add_fusion.ids_ref
  97.7 20.8 %attend.1 = (bf16[12,144,256]{2,1,0:T(8,128)(2,1)}, f32[12,8,256]{2,1,0:T(8,128)}, bf16[8,144,384]{2,1,0:T(8,128)(2,1)}) custom-call(s32[3]{0:T(128)} %pad_add_fusion.ids_ref, s32[8,128]{1,0:T(8,128)} %get-tuple-element.72.info_ref, s32[8,16]{1,0:T(8,128)} %bitcast.16, bf16[12,256,768]{2,1,0:T(8,128)(2,1)} %get-tuple-element.73.qkv_ref), custom_call_target="tpu_custom_call" | custom-call | flops 4831838208 | bytes 6590988 | tf_op jit(solution)/shard_map/attend/pallas_call | solution.py:32
  118.5 6.3 %collective-permute-done.1.refs_3_.refs_7_ = bf16[576,1152]{1,0:T(8,128)(2,1)S(1)} collective-permute-done((bf16[576,1152]{1,0:T(8,128)(2,1)}, bf16[576,1152]{1,0:T(8,128)(2,1)S(1)}, u32[]{:S(2)}, u32[]{:S(2)}) %collective-permute-start.1) | collective-permute-done | bytes 1327136 | tf_op jit(solution)/shard_map/ppermute | solution.py:51
  124.8 0.4 collective-permute-done.refs_2_.refs_6_
  125.1 0.7 copy-done.2
  125.8 37.3 %project.1 = (f32[384,1152]{1,0:T(8,128)}, f32[384,1152]{1,0:T(8,128)}, bf16[2,384,1152]{2,1,0:T(8,128)(2,1)}, bf16[1152,384]{1,0:T(8,128)(2,1)}, bf16[1,288,115...) custom-call(f32[16,6912]{1,0:T(8,128)} %get-tuple-element.68.mod_ref, ...), custom_call_target="tpu_custom_call" | custom-call | flops 1019215872 | bytes 19021824 | tf_op jit(solution)/shard_map/project/pallas_call | solution.py:32
  163.2 39.0 %feed_forward.1 = (f32[384,1152]{1,0:T(8,128)}, bf16[384,1152]{1,0:T(8,128)(2,1)}, f32[384,1152]{1,0:T(8,128)}, bf16[384,1152]{1,0:T(8,128)(2,1)}, bf16[4,1152,1152]{2,1,0:T(8,128)(2,1)}) custom-call(s32[3]{0:T(128)} %pad_add_fusion.ids_ref, f32[2,8,384]{2,1,0:T(8,128)} %get-tuple-element.85.hot_ref, s32[8,2304]{1,0:T(8,128)} %reshape.45.chan_ref, ...), custom_call_target="tpu_custom_call" | custom-call | flops 24461180928 | bytes 30179340 | tf_op jit(solution)/shard_map/feed_forward/pallas_call | solution.py:32
  202.2 0.0 reduce-scatter.2.cloned.1.call-update
  202.2 33.3 %middle_back.1 = (bf16[8,144,384]{2,1,0:T(8,128)(2,1)}, f32[384,1152]{1,0:T(8,128)}, f32[8,2304]{1,0:T(8,128)}, f32[8,2304]{1,0:T(8,128)}, bf16[384,1152]{1,0:T(...) custom-call(f32[16,6912]{1,0:T(8,128)} %get-tuple-element.68.mod_ref, ...), custom_call_target="tpu_custom_call" | custom-call | flops 2038431744 | bytes 20353024 | tf_op jit(solution)/shard_map/middle_back/pallas_call | solution.py:32
  235.5 29.6 %attend_back.1.d_ref = bf16[12,256,768]{2,1,0:T(8,128)(2,1)} custom-call(s32[3]{0:T(128)} %pad_add_fusion.ids_ref, s32[8,128]{1,0:T(8,128)} %get-tuple-element.72.info_ref, s32[8,16]{1,0:T(8,128)} %bitcast.17, bf16[12,256,768]{2,1,0:T(8,128)(2,1)} %get-tuple-element.73.qkv_ref, bf16[12,144,256]{2,1,0:T(8,128)(2,1)} %get-tuple-element.103.o_ref, ...), custom_call_target="tpu_custom_call" | custom-call | flops 12079595520 | bytes 11309580 | tf_op jit(solution)/shard_map/attend_back/pallas_call | solution.py:32
  265.1 81.3 %stream_back.1 = (bf16[384,1152]{1,0:T(8,128)(2,1)}, f32[8,2304]{1,0:T(8,128)}, bf16[288,432]{1,0:T(8,128)(2,1)}, bf16[144,1152]{1,0:T(8,128)(2,1)}) custom-call(bf16[12,256,1152]{2,1,0:T(8,128)(2,1)} %get-tuple-element.101.h_ref, bf16[4,144,1152]{2,1,0:T(8,128)(2,1)} %get-tuple-element.102.gs_ref, bf16[12,256,768]{2,1,0:T(8,128)(2,1)} %attend_back.1.d_ref, ...), custom_call_target="tpu_custom_call" | custom-call | flops 10871635968 | bytes 21154816 | tf_op jit(solution)/shard_map/stream_back/pallas_call | solution.py:32
  346.4 0.0 reduce-scatter.2.cloned.1.call-done
  346.4 114.9 %finish.1 = (bf16[2,9,144,1152]{3,2,1,0:T(8,128)(2,1)}, bf16[8,288,432]{2,1,0:T(8,128)(2,1)}, f32[4,8,6912]{2,1,0:T(8,128)}, f32[4,32,288]{2,1,0:T(8,128)}) custom-call(bf16[8,144,1152]{2,1,0:T(8,128)(2,1)} %bitcast.14, bf16[288,6912]{1,0:T(8,128)(2,1)} %ada_ref.3, bf16[144,1152]{1,0:T(8,128)(2,1)} %get-tuple-element.112.go_ref, ...), custom_call_target="tpu_custom_call" | custom-call | bytes 16468992 | tf_op jit(solution)/shard_map/finish/pallas_call | solution.py:32
  461.3 12.2 %unfold.1 = (f32[64,1152]{1,0:T(8,128)}, f32[288,6912]{1,0:T(8,128)}, f32[288,3456]{1,0:T(8,128)}, f32[288,1152]{1,0:T(8,128)}, f32[288,4608]{1,0:T(8,128)}, /*index=5*/f32[1152,1152]{1,0:T(8,128)}) custom-call(bf16[32,288]{1,0:T(8,128)(2,1)} %get-tuple-element.109.low_ref, f32[32,64]{1,0:T(8,128)} %get-tuple-element.110.wave_ref, ...), custom_call_target="tpu_custom_call" | custom-call | bytes 33204224 | tf_op jit(solution)/shard_map/unfold/pallas_call | solution.py:32
  473.5 0.0 copy-start.1
  473.5 0.9 copy.25
  474.4 0.5 copy-done.4
  475.0 0.9 copy.26
  (8 shorter events, 0.0 us)
Async XLA Ops:
  7.2 2.0 copy-start
  7.2 339.3 %reduce-scatter.2.cloned.1.call-start = ((), (), s32[]{:S(2)}) async-start(), calls=%async_computation.1 | async-start | bytes 13271040 | tf_op jit(solution)/shard_map/reduce_scatter | solution.py:1459
  10.4 85.5 %copy-start.5 = (s32[1,8,4608]{2,1,0:T(8,128)S(1)}, s32[1,8,4608]{2,1,0:T(8,128)}, u32[]{:S(2)}) copy-start(s32[1,8,4608]{2,1,0:T(8,128)} %param.17) | copy-start | bytes 442372
  93.9 30.9 %collective-permute-start.1 = (bf16[576,1152]{1,0:T(8,128)(2,1)}, bf16[576,1152]{1,0:T(8,128)(2,1)S(1)}, u32[]{:S(2)}, u32[]{:S(2)}) collective-permute-start(bf16[576,1152]{1,0:T(8,128)(2,1)} %get-tuple-element.77.refs_5_), channel_id=1, source_target_pairs={{0,16},{8,24},{16,0},{24,8},{1,17},{9,25},{17,1},{25,9},{2,18},{10... | collective-permute-start | bytes 3981320 | tf_op jit(solution)/shard_map/ppermute | solution.py:51
  94.3 30.8 %collective-permute-start = (bf16[576,1152]{1,0:T(8,128)(2,1)}, bf16[576,1152]{1,0:T(8,128)(2,1)}, u32[]{:S(2)}, u32[]{:S(2)}) collective-permute-start(bf16[576,1152]{1,0:T(8,128)(2,1)} %get-tuple-element.77.refs_5_), channel_id=1, source_target_pairs={{0,8},{8,0},{16,24},{24,16},{1,9},{9,1},{17,25},{25,17},{2,10},{10... | collective-permute-start | bytes 3981320 | tf_op jit(solution)/shard_map/ppermute | solution.py:51
  124.8 1.1 copy-start.2
  461.3 12.2 %copy-start.3 = (bf16[384,1152]{1,0:T(8,128)(2,1)S(1)}, bf16[384,1152]{1,0:T(8,128)(2,1)}, u32[]{:S(2)}) copy-start(bf16[384,1152]{1,0:T(8,128)(2,1)} %get-tuple-element.138) | copy-start | bytes 2654212
  473.5 1.5 copy-start.4
  473.5 2.4 copy-start.1
Sparse Core Ops, SparseCore 0:
  202.3 121.2 reduce-scatter.1
